TPU v7x, 512 devices: a whole 4x8x8 slice. The times are simulated.
512 devices in a mesh: dp: 64 (over z, y), mp: 8 (over x, core).
Axes of the slice: x: 4, y: 8, z: 8, core: 2. Of those that a mesh axis runs over, the one named last changes fastest.
Arguments:
- spikes: bfloat16 [3584, 16, 384], P('dp'), may hold values from -6 to 6
- session_ids: int32 [3584, 1], P('dp'), may hold values from 0 to 63; in each aligned block of 56 rows (0 to 55, 56 to 111, ...) at most 2 rows name the same one
- readin: bfloat16 [64, 384, 4096], P('dp', None, 'mp')
- gain: float32 [4096], P('mp'), may hold values from 0.5 to 1.5
- proj: bfloat16 [4096, 2048], P('mp', 'dp'), may hold values from -0.09375 to 0.09375
- query_bias: float32 [2048], P('mp'), may hold values from -1.5 to 1.5
- cotangent: bfloat16 [3584, 16, 2048], P('dp', None, 'mp'), may hold values from -0.0234375 to 0.0234375
Outputs:
- readin_grad: float32 [64, 384, 4096], P('dp', None, 'mp')
- gain_grad: float32 [4096], P('mp')
- proj_grad: float32 [4096, 2048], P('mp', 'dp')
Inputs may be any that keep to these rules, and one draw needn't show every extreme that they name: `session_ids`: among the 56 windows of one device no session appears more than 2 times, and some session appears exactly 2 times.
All inputs are finite; a program needn't handle non-finite values.
Results may differ from a plain program's by a relative error of at most 0.011.
Values may be sent and summed in bfloat16 or wider, within the bound.
A program may use at most 64 MiB of HBM per device.

v0:
```python
import jax
import jax.numpy as jnp
from jax import lax
from jax.sharding import PartitionSpec as P

D = 4096
HD = 128
MOST = 2
eps_norm = 1e-05


def on_device(spikes, session_ids, readin, gain, proj, query_bias, cotangent):
    windows, bin_count, channels = spikes.shape
    owner_count = lax.axis_size("dp")
    slot_count = owner_count * MOST
    slice_width = readin.shape[2]
    row_count = windows * bin_count
    share = cotangent.shape[2]
    owners = session_ids[:, 0]
    positions = jnp.arange(windows)
    earlier = (owners[:, None] == owners[None, :]) & (positions[None, :] < positions[:, None])
    ranked = jnp.sum(earlier.astype(jnp.int32), axis=1)
    target = owners * MOST + ranked
    placing = (jnp.arange(slot_count)[:, None] == target[None, :]).astype(jnp.bfloat16)
    outgoing = jnp.dot(
        placing, spikes.reshape(windows, bin_count * channels), preferred_element_type=jnp.float32
    )
    outgoing = outgoing.astype(jnp.bfloat16).reshape(owner_count, MOST, bin_count, channels)
    table = readin[0]
    arrived = lax.all_to_all(outgoing, "dp", split_axis=0, concat_axis=0, tiled=True)
    items = arrived.shape[1]
    mapped = jnp.dot(arrived.reshape(-1, channels), table, preferred_element_type=jnp.float32)
    mapped = mapped.astype(jnp.bfloat16).reshape(owner_count, items, bin_count, slice_width)
    returned = lax.all_to_all(mapped, "dp", split_axis=0, concat_axis=0, tiled=True)
    returned, arrived = (returned, arrived)
    gathered_rows = lax.dot_general(
        placing,
        returned.reshape(slot_count, bin_count * slice_width),
        (((0,), (0,)), ((), ())),
        preferred_element_type=jnp.float32,
    )
    features = gathered_rows.reshape(row_count, slice_width)
    squares = lax.psum(jnp.sum(features * features, axis=-1), "mp")
    inverse = lax.rsqrt(squares / D + eps_norm)[:, None]
    normed = (features * inverse * gain).astype(jnp.bfloat16)
    whole_proj = lax.all_gather(proj, "dp", axis=1, tiled=True)
    partial_queries = jnp.dot(normed, whole_proj, preferred_element_type=jnp.float32)
    summed = lax.psum(partial_queries.astype(jnp.bfloat16), "mp").astype(jnp.float32)
    own_queries = lax.dynamic_slice_in_dim(summed, lax.axis_index("mp") * share, share, 1)
    own_queries = own_queries + query_bias
    queries = own_queries.reshape(row_count, share // HD, HD)
    scale = lax.rsqrt(jnp.mean(queries * queries, axis=-1, keepdims=True) + eps_norm)
    unit = queries * scale
    upstream = cotangent.reshape(row_count, share // HD, HD).astype(jnp.float32)
    own_grad = scale * (upstream - unit * jnp.mean(upstream * unit, axis=-1, keepdims=True))
    own_grad = own_grad.reshape(row_count, share).astype(jnp.bfloat16)
    query_grad = lax.all_gather(own_grad, "mp", axis=1, tiled=True)
    proj_grad = lax.psum_scatter(
        lax.dot_general(
            query_grad, normed, (((0,), (0,)), ((), ())), preferred_element_type=jnp.float32
        ),
        "dp",
        scatter_dimension=0,
        tiled=True,
    ).T
    normed_grad = lax.dot_general(
        query_grad, whole_proj, (((1,), (1,)), ((), ())), preferred_element_type=jnp.float32
    )
    scaled_grad = gain * normed_grad
    cross_sums = lax.psum(jnp.sum(scaled_grad * features, axis=-1), "mp")
    feature_grad = inverse * scaled_grad - features * inverse**3 * (cross_sums / D)[:, None]
    feature_grad = feature_grad.astype(jnp.bfloat16).reshape(windows, bin_count * slice_width)
    local_gain = jnp.sum(normed_grad * features * inverse, axis=0)
    gain_grad = lax.psum(local_gain, "dp")
    slotted = jnp.dot(placing, feature_grad, preferred_element_type=jnp.float32)
    slotted = slotted.astype(jnp.bfloat16).reshape(owner_count, MOST, bin_count, slice_width)
    incoming = lax.all_to_all(slotted, "dp", split_axis=0, concat_axis=0, tiled=True)
    readin_grad = lax.dot_general(
        arrived.reshape(-1, channels),
        incoming.reshape(-1, slice_width),
        (((0,), (0,)), ((), ())),
        preferred_element_type=jnp.float32,
    )
    return (readin_grad[None], gain_grad, proj_grad)


def solution(mesh):
    return jax.shard_map(
        on_device,
        mesh=mesh,
        in_specs=(
            P("dp", None, None),
            P("dp", None),
            P("dp", None, "mp"),
            P("mp"),
            P("mp", "dp"),
            P("mp"),
            P("dp", None, "mp"),
        ),
        out_specs=(P("dp", None, "mp"), P("mp"), P("mp", "dp")),
        check_vma=False,
    )
```

profile of v0, /device:TPU:2, one launch (start us, length us, event | category | flops | bytes accessed | tf_op | source)
XLA Modules:
  0.0 636.0 jit_solution(13360322924819784834)
XLA Ops:
  7.2 0.9 convert_reduce_fusion
  8.8 1.2 copy.18
  10.9 57.7 %all_to_all.15 = bf16[64,2,16,384]{3,2,1,0:T(8,128)(2,1)S(1)} all-to-all(bf16[64,2,16,384]{3,2,1,0:T(8,128)(2,1)S(1)} %bitcast.56), channel_id=1, replica_groups=mesh['dp'=64,'mp'=8] {'dp'}, dimensions={0} | all-to-all | bytes 3145728 | tf_op jit(solution)/shard_map/all_to_all | solution.py:30
  68.5 2.6 convolution_convert_fusion.3
  71.2 7.6 %all-to-all-start.1 = ((bf16[64,2,16,512]{3,2,1,0:T(8,128)(2,1)}), bf16[64,2,16,512]{3,2,1,0:T(8,128)(2,1)S(1)}, u32[]{:S(2)}, u32[]{:S(2)}) async-start(bf16[64,2,16,512]{3,2,1,0:T(8,128)(2,1)} %bitcast.60), calls=%async_computation.1 | async-start | bytes 4194304 | tf_op jit(solution)/shard_map/all_to_all | solution.py:34
  79.5 51.1 %all-to-all-done.1 = bf16[64,2,16,512]{3,2,1,0:T(8,128)(2,1)S(1)} async-done(((bf16[64,2,16,512]{3,2,1,0:T(8,128)(2,1)}), bf16[64,2,16,512]{3,2,1,0:T(8,128)(2,1)S(1)}, u32[]{:S(2)}, u32[]{:S(2)}) %all-to-all-start.1) | async-done | bytes 2097184 | tf_op jit(solution)/shard_map/all_to_all | solution.py:34
  130.7 1.4 copy.20
  132.0 1.7 fusion.4
  133.8 1.6 reshape.78
  135.6 10.4 %psum.28 = f32[896]{0:T(1024)S(1)} all-reduce(f32[896]{0:T(1024)S(1)} %multiply_reduce_fusion.2), channel_id=1, replica_groups=mesh['dp'=64,'mp'=8] {'mp'}, use_global_device_ids=true, to_apply=%region_2.0 | all-reduce | flops 896 | bytes 7168 | tf_op jit(solution)/shard_map/psum | solution.py:43
  146.0 39.0 %all-gather.3.cloned.1.call-done = bf16[512,2048]{0,1:T(8,128)(2,1)} async-done(((bf16[512,32]{0,1:T(8,128)(2,1)}), bf16[512,2048]{0,1:T(8,128)(2,1)}) %all-gather.3.cloned.1.call-update) | async-done | bytes 2097168 | tf_op jit(solution)/shard_map/all_gather | solution.py:46
  185.0 5.6 convolution_convert_fusion.2
  190.8 0.8 copy-done.2
  191.6 1.4 reshape.83
  193.0 73.4 %all-reduce.2.cloned.1.call-done = bf16[896,2048]{1,0:T(8,128)(2,1)} async-done(((bf16[896,2048]{1,0:T(8,128)(2,1)}), bf16[896,2048]{1,0:T(8,128)(2,1)}) %all-reduce.2.cloned.1.call-update) | async-done | bytes 3670032 | tf_op jit(solution)/shard_map/psum | solution.py:48
  266.4 2.0 convert_add_fusion
  268.4 1.6 reshape.79
  270.1 1.0 multiply_reduce_fusion.4
  271.3 12.7 %multiply_reduce_fusion.3 = f32[896,2]{1,0:T(8,128)S(1)} fusion(f32[896,2,128]{2,1,0:T(2,128)S(1)} %copy-done.1, f32[896,2,128]{2,1,0:T(2,128)S(1)} %reshape.79, f32[896,2]{1,0:T(8,128)S(1)} %add_rsqrt_fusion), kind=kLoop, calls=%fused_computation.15 | loop fusion | flops 686336 | bytes 1849344 | tf_op jit(solution)/shard_map/reduce_sum | solution.py:55
  284.0 1.1 mul.123
  285.1 1.1 mul.118
  286.2 2.1 fusion.2
  288.3 41.5 %all-gather.5.cloned.1.call-done = bf16[896,2048]{1,0:T(8,128)(2,1)} async-done(((bf16[896,256]{1,0:T(8,128)(2,1)}), bf16[896,2048]{1,0:T(8,128)(2,1)}) %all-gather.5.cloned.1.call-update) | async-done | bytes 3670032 | tf_op jit(solution)/shard_map/all_gather | solution.py:57
  329.8 6.4 %fusion.9 = f32[2048,512]{1,0:T(8,128)} fusion(bf16[896,2048]{1,0:T(8,128)(2,1)} %all-gather.5.cloned.1.call-done, f32[896,512]{1,0:T(8,128)S(1)} %reshape.78, f32[512]{0:T(512)S(1)} %copy-done.6, f32[896]{0:T(1024)S(1)} %get-tuple-element.6), kind=kOutput, calls=%fused_computation.33 | convolution fusion | flops 1880424448 | bytes 9704960 | tf_op jit(solution)/shard_map/dot_general | solution.py:59
  336.3 6.1 multiply_reduce_fusion
  342.4 12.0 %psum.30 = f32[896]{0:T(1024)S(1)} all-reduce(f32[896]{0:T(1024)S(1)} %get-tuple-element.4), channel_id=1, replica_groups=mesh['dp'=64,'mp'=8] {'mp'}, use_global_device_ids=true, to_apply=%region_7.0 | all-reduce | flops 896 | bytes 7168 | tf_op jit(solution)/shard_map/psum | solution.py:70
  354.4 1.9 subtract_convert_fusion
  357.4 2.2 copy.23
  359.6 13.3 %all-to-all-start.2 = ((bf16[64,2,16,512]{3,2,1,0:T(8,128)(2,1)}), bf16[64,2,16,512]{3,2,1,0:T(8,128)(2,1)S(1)}, u32[]{:S(2)}, u32[]{:S(2)}) async-start(bf16[64,2,16,512]{3,2,1,0:T(8,128)(2,1)} %bitcast.25), calls=%async_computation.2 | async-start | bytes 4194304 | tf_op jit(solution)/shard_map/all_to_all | solution.py:77
  372.9 181.6 %psum.31 = f32[512]{0:T(512)} all-reduce(f32[512]{0:T(512)S(1)} %get-tuple-element.3), channel_id=1, replica_groups=mesh['dp'=64,'mp'=8] {'dp'}, use_global_device_ids=true, to_apply=%region_9.0 | all-reduce | flops 512 | bytes 4096 | tf_op jit(solution)/shard_map/psum | solution.py:74
  554.5 3.3 convolution_bitcast_fusion
  557.8 71.7 %reduce-scatter.2.cloned.1.call-done = f32[32,512]{1,0:T(8,128)} async-done(((f32[2048,512]{1,0:T(8,128)}), f32[32,512]{1,0:T(8,128)}) %reduce-scatter.2.cloned.1.call-update) | async-done | bytes 65552 | tf_op jit(solution)/shard_map/reduce_scatter | solution.py:58
  (32 shorter events, 4.1 us)
Async XLA Ops:
  7.2 61.4 %copy-start = (bf16[1,384,512]{2,1,0:T(8,128)(2,1)S(1)}, bf16[1,384,512]{2,1,0:T(8,128)(2,1)}, u32[]{:S(2)}) copy-start(bf16[1,384,512]{2,1,0:T(8,128)(2,1)} %param.9) | copy-start | bytes 1179652
  68.5 2.6 copy-start.4
  71.2 59.5 %all-to-all-start.1 = ((bf16[64,2,16,512]{3,2,1,0:T(8,128)(2,1)}), bf16[64,2,16,512]{3,2,1,0:T(8,128)(2,1)S(1)}, u32[]{:S(2)}, u32[]{:S(2)}) async-start(bf16[64,2,16,512]{3,2,1,0:T(8,128)(2,1)} %bitcast.60), calls=%async_computation.1 | async-start | bytes 4194304 | tf_op jit(solution)/shard_map/all_to_all | solution.py:34
  78.8 106.3 %all-gather.3.cloned.1.call-start = ((), (), s32[]{:S(2)}) async-start(), calls=%async_computation.4 | async-start | bytes 2129920 | tf_op jit(solution)/shard_map/all_gather | solution.py:46
  79.5 186.9 %all-reduce.2.cloned.1.call-start = ((), (), s32[]{:S(2)}) async-start(), calls=%async_computation.5 | async-start | bytes 7340032 | tf_op jit(solution)/shard_map/psum | solution.py:48
  135.4 49.6 %copy-start.6 = (f32[512]{0:T(512)S(1)}, f32[512]{0:T(512)}, u32[]{:S(2)}) copy-start(f32[512]{0:T(512)} %param.10) | copy-start | bytes 6148
  190.6 1.0 copy-start.2
  190.6 75.8 %copy-start.5 = (f32[256]{0:T(256)S(1)}, f32[256]{0:T(256)}, u32[]{:S(2)}) copy-start(f32[256]{0:T(256)} %param.12) | copy-start | bytes 3076
  190.6 139.2 %all-gather.5.cloned.1.call-start = ((), (), s32[]{:S(2)}) async-start(), calls=%async_computation.6 | async-start | bytes 4128768 | tf_op jit(solution)/shard_map/all_gather | solution.py:57
  270.1 1.2 copy-start.1
  283.9 2.3 copy-start.3
  288.3 341.2 %reduce-scatter.2.cloned.1.call-start = ((), (), s32[]{:S(2)}) async-start(), calls=%async_computation.7 | async-start | bytes 4259840 | tf_op jit(solution)/shard_map/reduce_scatter | solution.py:58
  359.6 194.9 %all-to-all-start.2 = ((bf16[64,2,16,512]{3,2,1,0:T(8,128)(2,1)}), bf16[64,2,16,512]{3,2,1,0:T(8,128)(2,1)S(1)}, u32[]{:S(2)}, u32[]{:S(2)}) async-start(bf16[64,2,16,512]{3,2,1,0:T(8,128)(2,1)} %bitcast.25), calls=%async_computation.2 | async-start | bytes 4194304 | tf_op jit(solution)/shard_map/all_to_all | solution.py:77
Sparse Core Ops, SparseCore 0:
  82.7 102.3 all-gather.2
  190.7 75.6 all-reduce.1
  288.4 41.3 all-gather.4
  336.4 293.0 reduce-scatter.1
where the time goes:
time: 637 us; the launch traced here: 636 us
  waiting for transfers between devices  277 us (43%)
  blocking collectives  262 us (41%)
  matrix products  27 us (4%)
  other arithmetic  21.6 us (3%)
  starting transfers between devices  21.2 us (3%)
  between operations  13.9 us (2%)
  local copies, waits for them, and re-layouts  13.2 us (2%)
    psum x1, blocking collectives, on_device(): gain_grad = lax.psum(local_gain, 'dp')  182 us
    psum x1, waiting for transfers between devices, on_device(): lax.psum(partial_queries.astype(jnp.bfloat16), 'mp').astype(jnp.float32)  73.4 us
    reduce_scatter x1, waiting for transfers between devices, on_device(): lax.psum_scatter(lax.dot_general(query_grad, normed, (((0,), (0,)), ((),...  71.7 us
    all_to_all x1, blocking collectives, on_device(): lax.all_to_all(outgoing, 'dp', split_axis=0, concat_axis=0, tiled=True)  57.7 us
    all_to_all x1, waiting for transfers between devices, on_device(): lax.all_to_all(mapped, 'dp', split_axis=0, concat_axis=0, tiled=True)  51.1 us
    all_gather x1, waiting for transfers between devices, on_device(): query_grad = lax.all_gather(own_grad, 'mp', axis=1, tiled=True)  41.5 us
    all_gather x1, waiting for transfers between devices, on_device(): whole_proj = lax.all_gather(proj, 'dp', axis=1, tiled=True)  39 us
    all_to_all x1, starting transfers between devices, on_device(): lax.all_to_all(slotted, 'dp', split_axis=0, concat_axis=0, tiled=True)  13.3 us
  transfers between devices with their start and end apart: 6, of which 5 were waited for; matrix products, arithmetic and copies ran while one was open for 3% of the time, Pallas kernels for 0%

commit v1 on v0

--- a/solution.py
+++ b/solution.py
@@ -10,6 +10,11 @@
 
 
 def on_device(spikes, session_ids, readin, gain, proj, query_bias, cotangent):
+
+    def follow_the_arrays(sample, mesh_ax):
+        block_last = lax.all_gather(sample, axis_name=mesh_ax)
+        return jnp.sum(block_last, 0)
+
     windows, bin_count, channels = spikes.shape
     owner_count = lax.axis_size("dp")
     slot_count = owner_count * MOST
@@ -45,7 +50,7 @@
     normed = (features * inverse * gain).astype(jnp.bfloat16)
     whole_proj = lax.all_gather(proj, "dp", axis=1, tiled=True)
     partial_queries = jnp.dot(normed, whole_proj, preferred_element_type=jnp.float32)
-    summed = lax.psum(partial_queries.astype(jnp.bfloat16), "mp").astype(jnp.float32)
+    summed = follow_the_arrays(partial_queries.astype(jnp.bfloat16), "mp").astype(jnp.float32)
     own_queries = lax.dynamic_slice_in_dim(summed, lax.axis_index("mp") * share, share, 1)
     own_queries = own_queries + query_bias
     queries = own_queries.reshape(row_count, share // HD, HD)

time: 637 us -> 711 us (1.12)
  waiting for transfers between devices: 277 us -> 338 us
  other arithmetic: 21.6 us -> 34.3 us
    all_gather x0 -> x1, waiting for transfers between devices: none -> 138 us  [follow_the_arrays(): block_last = lax.all_gather(sample, axis_name=mesh_ax)]
    psum x1 -> x0, waiting for transfers between devices: 73.4 us -> none  [on_device(): lax.psum(partial_queries.astype(jnp.bfloat16), 'mp').astype(jnp.float32)]
    reduce_sum x0 -> x1, other arithmetic: none -> 12.7 us  [follow_the_arrays(): return jnp.sum(block_last, 0)]
where the time goes in v1:
time: 711 us; the launch traced here: 710 us
  waiting for transfers between devices  338 us (48%)
  blocking collectives  262 us (37%)
  other arithmetic  34.3 us (5%)
  matrix products  27.1 us (4%)
  starting transfers between devices  21.2 us (3%)
  between operations  13.9 us (2%)
  local copies, waits for them, and re-layouts  13.2 us (2%)
    psum x1, blocking collectives, on_device(): gain_grad = lax.psum(local_gain, 'dp')  182 us
    all_gather x1, waiting for transfers between devices, follow_the_arrays(): block_last = lax.all_gather(sample, axis_name=mesh_ax)  138 us
    reduce_scatter x1, waiting for transfers between devices, on_device(): lax.psum_scatter(lax.dot_general(query_grad, normed, (((0,), (0,)), ((),...  69.7 us
    all_to_all x1, blocking collectives, on_device(): lax.all_to_all(outgoing, 'dp', split_axis=0, concat_axis=0, tiled=True)  57.7 us
    all_to_all x1, waiting for transfers between devices, on_device(): lax.all_to_all(mapped, 'dp', split_axis=0, concat_axis=0, tiled=True)  51 us
    all_gather x1, waiting for transfers between devices, on_device(): query_grad = lax.all_gather(own_grad, 'mp', axis=1, tiled=True)  39.9 us
    all_gather x1, waiting for transfers between devices, on_device(): whole_proj = lax.all_gather(proj, 'dp', axis=1, tiled=True)  39 us
  transfers between devices with their start and end apart: 6, of which 5 were waited for; matrix products, arithmetic and copies ran while one was open for 3% of the time, Pallas kernels for 0%

profile of v1, /device:TPU:2, one launch (start us, length us, event | category | flops | bytes accessed | tf_op | source)
XLA Modules:
  0.0 710.0 jit_solution(6636761314439321243)
XLA Ops:
  7.2 0.9 convert_reduce_fusion
  8.8 1.2 copy.18
  10.9 57.7 %all_to_all.15 = bf16[64,2,16,384]{3,2,1,0:T(8,128)(2,1)S(1)} all-to-all(bf16[64,2,16,384]{3,2,1,0:T(8,128)(2,1)S(1)} %bitcast.58), channel_id=1, replica_groups=mesh['dp'=64,'mp'=8] {'dp'}, dimensions={0} | all-to-all | bytes 3145728 | tf_op jit(solution)/shard_map/all_to_all | solution.py:35
  68.5 2.6 convolution_convert_fusion.3
  71.2 7.6 %all-to-all-start.1 = ((bf16[64,2,16,512]{3,2,1,0:T(8,128)(2,1)}), bf16[64,2,16,512]{3,2,1,0:T(8,128)(2,1)S(1)}, u32[]{:S(2)}, u32[]{:S(2)}) async-start(bf16[64,2,16,512]{3,2,1,0:T(8,128)(2,1)} %bitcast.62), calls=%async_computation.1 | async-start | bytes 4194304 | tf_op jit(solution)/shard_map/all_to_all | solution.py:39
  79.5 51.0 %all-to-all-done.1 = bf16[64,2,16,512]{3,2,1,0:T(8,128)(2,1)S(1)} async-done(((bf16[64,2,16,512]{3,2,1,0:T(8,128)(2,1)}), bf16[64,2,16,512]{3,2,1,0:T(8,128)(2,1)S(1)}, u32[]{:S(2)}, u32[]{:S(2)}) %all-to-all-start.1) | async-done | bytes 2097184 | tf_op jit(solution)/shard_map/all_to_all | solution.py:39
  130.6 1.4 copy.20
  132.0 1.7 fusion.4
  133.7 1.6 reshape.78
  135.6 10.5 %psum.21 = f32[896]{0:T(1024)S(1)} all-reduce(f32[896]{0:T(1024)S(1)} %multiply_reduce_fusion.2), channel_id=1, replica_groups=mesh['dp'=64,'mp'=8] {'mp'}, use_global_device_ids=true, to_apply=%region_2.0 | all-reduce | flops 896 | bytes 7168 | tf_op jit(solution)/shard_map/psum | solution.py:48
  146.1 39.0 %all-gather.5.cloned.1.call-done = bf16[512,2048]{0,1:T(8,128)(2,1)} async-done(((bf16[512,32]{0,1:T(8,128)(2,1)}), bf16[512,2048]{0,1:T(8,128)(2,1)}) %all-gather.5.cloned.1.call-update) | async-done | bytes 2097168 | tf_op jit(solution)/shard_map/all_gather | solution.py:51
  185.1 5.5 convolution_convert_fusion.2
  191.6 1.4 reshape.83
  193.1 138.0 %all-gather.9.cloned.1.call-done = bf16[7168,2048]{1,0:T(8,128)(2,1)} async-done(((bf16[896,2048]{1,0:T(8,128)(2,1)}), bf16[7168,2048]{1,0:T(8,128)(2,1)}) %all-gather.9.cloned.1.call-update) | async-done | bytes 29360144 | tf_op jit(solution)/shard_map/all_gather | solution.py:15
  331.0 12.7 %reduce_sum.68 = bf16[896,2048]{1,0:T(8,128)(2,1)} reduce(bf16[8,896,2048]{2,1,0:T(8,128)(2,1)} %bitcast.53, bf16[]{:T(256)} %constant.22.clone.1), dimensions={0}, to_apply=%region_3.0 | reduce | flops 12845056 | bytes 33030146 | tf_op jit(solution)/shard_map/reduce_sum | solution.py:16
  343.7 2.0 convert_add_fusion
  345.7 1.6 reshape.79
  347.4 1.0 multiply_reduce_fusion.4
  348.5 12.7 %multiply_reduce_fusion.3 = f32[896,2]{1,0:T(8,128)S(1)} fusion(f32[896,2,128]{2,1,0:T(2,128)S(1)} %copy-done.2, f32[896,2,128]{2,1,0:T(2,128)S(1)} %reshape.79, f32[896,2]{1,0:T(8,128)S(1)} %add_rsqrt_fusion), kind=kLoop, calls=%fused_computation.15 | loop fusion | flops 686336 | bytes 1849344 | tf_op jit(solution)/shard_map/reduce_sum | solution.py:60
  361.2 1.1 mul.123
  362.4 1.1 mul.118
  363.5 2.1 fusion.2
  365.6 39.9 %all-gather.7.cloned.1.call-done = bf16[896,2048]{1,0:T(8,128)(2,1)} async-done(((bf16[896,256]{1,0:T(8,128)(2,1)}), bf16[896,2048]{1,0:T(8,128)(2,1)}) %all-gather.7.cloned.1.call-update) | async-done | bytes 3670032 | tf_op jit(solution)/shard_map/all_gather | solution.py:62
  405.6 6.4 fusion.9
  412.0 6.2 multiply_reduce_fusion
  418.2 11.9 %psum.22 = f32[896]{0:T(1024)S(1)} all-reduce(f32[896]{0:T(1024)S(1)} %get-tuple-element.4), channel_id=1, replica_groups=mesh['dp'=64,'mp'=8] {'mp'}, use_global_device_ids=true, to_apply=%region_7.0 | all-reduce | flops 896 | bytes 7168 | tf_op jit(solution)/shard_map/psum | solution.py:75
  430.2 1.9 subtract_convert_fusion
  433.3 2.2 copy.23
  435.4 13.3 %all-to-all-start.2 = ((bf16[64,2,16,512]{3,2,1,0:T(8,128)(2,1)}), bf16[64,2,16,512]{3,2,1,0:T(8,128)(2,1)S(1)}, u32[]{:S(2)}, u32[]{:S(2)}) async-start(bf16[64,2,16,512]{3,2,1,0:T(8,128)(2,1)} %bitcast.26), calls=%async_computation.2 | async-start | bytes 4194304 | tf_op jit(solution)/shard_map/all_to_all | solution.py:82
  448.7 181.7 %psum.23 = f32[512]{0:T(512)} all-reduce(f32[512]{0:T(512)S(1)} %get-tuple-element.3), channel_id=1, replica_groups=mesh['dp'=64,'mp'=8] {'dp'}, use_global_device_ids=true, to_apply=%region_9.0 | all-reduce | flops 512 | bytes 4096 | tf_op jit(solution)/shard_map/psum | solution.py:79
  630.4 3.4 convolution_bitcast_fusion
  633.8 69.7 %reduce-scatter.2.cloned.1.call-done = f32[32,512]{1,0:T(8,128)} async-done(((f32[2048,512]{1,0:T(8,128)}), f32[32,512]{1,0:T(8,128)}) %reduce-scatter.2.cloned.1.call-update) | async-done | bytes 65552 | tf_op jit(solution)/shard_map/reduce_scatter | solution.py:63
  (35 shorter events, 4.9 us)
Async XLA Ops:
  7.2 61.4 %copy-start = (bf16[1,384,512]{2,1,0:T(8,128)(2,1)S(1)}, bf16[1,384,512]{2,1,0:T(8,128)(2,1)}, u32[]{:S(2)}) copy-start(bf16[1,384,512]{2,1,0:T(8,128)(2,1)} %param.9) | copy-start | bytes 1179652
  68.5 2.6 copy-start.5
  71.2 59.4 %all-to-all-start.1 = ((bf16[64,2,16,512]{3,2,1,0:T(8,128)(2,1)}), bf16[64,2,16,512]{3,2,1,0:T(8,128)(2,1)S(1)}, u32[]{:S(2)}, u32[]{:S(2)}) async-start(bf16[64,2,16,512]{3,2,1,0:T(8,128)(2,1)} %bitcast.62), calls=%async_computation.1 | async-start | bytes 4194304 | tf_op jit(solution)/shard_map/all_to_all | solution.py:39
  78.8 106.3 %all-gather.5.cloned.1.call-start = ((), (), s32[]{:S(2)}) async-start(), calls=%async_computation.4 | async-start | bytes 2129920 | tf_op jit(solution)/shard_map/all_gather | solution.py:51
  79.5 251.5 %all-gather.9.cloned.1.call-start = ((), (), s32[]{:S(2)}) async-start(), calls=%async_computation.7 | async-start | bytes 33030144 | tf_op jit(solution)/shard_map/all_gather | solution.py:15
  135.3 49.8 %copy-start.7 = (f32[512]{0:T(512)S(1)}, f32[512]{0:T(512)}, u32[]{:S(2)}) copy-start(f32[512]{0:T(512)} %param.10) | copy-start | bytes 6148
  190.6 1.0 copy-start.3
  190.7 214.9 %all-gather.7.cloned.1.call-start = ((), (), s32[]{:S(2)}) async-start(), calls=%async_computation.5 | async-start | bytes 4128768 | tf_op jit(solution)/shard_map/all_gather | solution.py:62
  331.0 12.7 %copy-start.6 = (f32[256]{0:T(256)S(1)}, f32[256]{0:T(256)}, u32[]{:S(2)}) copy-start(f32[256]{0:T(256)} %param.12) | copy-start | bytes 3076
  347.4 1.2 copy-start.2
  361.2 2.3 copy-start.4
  365.6 337.9 %reduce-scatter.2.cloned.1.call-start = ((), (), s32[]{:S(2)}) async-start(), calls=%async_computation.6 | async-start | bytes 4259840 | tf_op jit(solution)/shard_map/reduce_scatter | solution.py:63
  435.4 195.0 %all-to-all-start.2 = ((bf16[64,2,16,512]{3,2,1,0:T(8,128)(2,1)}), bf16[64,2,16,512]{3,2,1,0:T(8,128)(2,1)S(1)}, u32[]{:S(2)}, u32[]{:S(2)}) async-start(bf16[64,2,16,512]{3,2,1,0:T(8,128)(2,1)} %bitcast.26), calls=%async_computation.2 | async-start | bytes 4194304 | tf_op jit(solution)/shard_map/all_to_all | solution.py:82
  630.4 73.0 %copy-start.1 = (bf16[1,384,512]{2,1,0:T(8,128)(2,1)S(1)}, bf16[1,384,512]{2,1,0:T(8,128)(2,1)}, u32[]{:S(2)}) copy-start(bf16[1,384,512]{2,1,0:T(8,128)(2,1)} %param.9) | copy-start | bytes 1179652
Sparse Core Ops, SparseCore 0:
  82.7 102.3 all-gather.4
  190.8 140.1 all-gather.8
  365.7 39.8 all-gather.6
  412.1 291.3 reduce-scatter.1
